TPU v7x, 32 devices: a whole 2x2x4 slice. The times are simulated.
32 devices in a mesh: rows: 8 (over z, x), pos: 4 (over y, core).
Axes of the slice: x: 2, y: 2, z: 4, core: 2. Of those that a mesh axis runs over, the one named last changes fastest.
Arguments:
- tokens: bfloat16 [24, 640, 768], P('rows', 'pos'), may hold values from -6 to 6
- segments: int32 [24, 640], P('rows'), may hold values from 0 to 7, as said below
- w_query: bfloat16 [768, 768], replicated, may hold values from -0.21875 to 0.21875
- b_query: bfloat16 [768], replicated, may hold values from -3 to 3
- w_key: bfloat16 [768, 768], replicated, may hold values from -0.21875 to 0.21875
- w_value: bfloat16 [768, 768], replicated, may hold values from -0.21875 to 0.21875
- b_value: bfloat16 [768], replicated, may hold values from -3 to 3
- w_out: bfloat16 [768, 768], replicated, may hold values from -0.875 to 0.875
- b_out: bfloat16 [768], replicated, may hold values from -3 to 3
- gain_one: bfloat16 [768], replicated, may hold values from 0.5 to 1.5
- shift_one: bfloat16 [768], replicated, may hold values from -3 to 3
- w_up: bfloat16 [768, 3072], replicated, may hold values from -0.21875 to 0.21875
- b_up: bfloat16 [3072], replicated, may hold values from -3 to 3
- w_down: bfloat16 [3072, 768], replicated, may hold values from -0.109375 to 0.109375
- b_down: bfloat16 [768], replicated, may hold values from -3 to 3
- gain_two: bfloat16 [768], replicated, may hold values from 0.5 to 1.5
- shift_two: bfloat16 [768], replicated, may hold values from -3 to 3
- cotangent: bfloat16 [24, 640, 768], P('rows', 'pos'), may hold values from -6 to 6
Outputs:
- result: bfloat16 [24, 640, 768], P('rows', 'pos')
- grad_tokens: float32 [24, 640, 768], P('rows', 'pos')
- grad_w_query: float32 [768, 768], replicated
- grad_b_query: float32 [768], replicated
- grad_w_key: float32 [768, 768], replicated
- grad_w_value: float32 [768, 768], replicated
- grad_b_value: float32 [768], replicated
- grad_w_out: float32 [768, 768], replicated
- grad_b_out: float32 [768], replicated
- grad_gain_one: float32 [768], replicated
- grad_shift_one: float32 [768], replicated
- grad_w_up: float32 [768, 3072], replicated
- grad_b_up: float32 [3072], replicated
- grad_w_down: float32 [3072, 768], replicated
- grad_b_down: float32 [768], replicated
- grad_gain_two: float32 [768], replicated
- grad_shift_two: float32 [768], replicated
Inputs may be any that keep to these rules, and one draw needn't show every extreme that they name: `segments`: each row's segment numbers start at 0, never fall, and rise by at most one from a position to the next.
All inputs are finite; a program needn't handle non-finite values.
Results may differ from a plain program's by a relative error of at most 0.014.
Values may be sent and summed in bfloat16 or wider, within the bound.
A program may use at most 192 MiB of HBM per device.

v0:
```python
from functools import partial

import jax
import jax.numpy as jnp
from jax import lax
from jax.experimental import pallas as pl
from jax.experimental.pallas import tpu as pltpu
from jax.sharding import PartitionSpec as P

HEADS = 12
HEAD_DIM = 64
EPS = 1e-05
MASKED = -1000000000.0
SCALE = HEAD_DIM ** (-0.5)
LANES = 128
VMEM_LIMIT = 60 * 2**20
MESH = pl.DeviceIdType.MESH
LOW = jnp.bfloat16
F32 = jnp.float32


def flip(value, bit):
    return value + bit - 2 * bit * lax.rem(lax.div(value, bit), 2)


def bit_of(value, bit):
    return lax.rem(lax.div(value, bit), 2)


def axis_bits(size):
    assert size & (size - 1) == 0
    return [1 << i for i in range(size.bit_length() - 1)]


def dot(a, b):
    return jnp.dot(a, b, preferred_element_type=F32)


def dot_nt(a, b):
    return lax.dot_general(a, b, (((1,), (1,)), ((), ())), preferred_element_type=F32)


def dot_tn(a, b):
    return lax.dot_general(a, b, (((0,), (0,)), ((), ())), preferred_element_type=F32)


class Place:
    def __init__(self):
        self.row = lax.axis_index("rows")
        self.pos = lax.axis_index("pos")

    def partner(self, link):
        axis, bit = link
        if axis == "r":
            return (flip(self.row, bit), self.pos)
        return (self.row, flip(self.pos, bit))

    def side(self, link):
        axis, bit = link
        return bit_of(self.row if axis == "r" else self.pos, bit)


def remote(src, dst, sems, index, device):
    send_sem, recv_sem = sems
    return pltpu.make_async_remote_copy(
        src_ref=src,
        dst_ref=dst,
        send_sem=send_sem.at[index],
        recv_sem=recv_sem.at[index],
        device_id=device,
        device_id_type=MESH,
    )


def greet(devices):
    barrier = pltpu.get_barrier_semaphore()
    for device in devices:
        pl.semaphore_signal(barrier, inc=1, device_id=device, device_id_type=MESH)
    pl.semaphore_wait(barrier, len(devices))


def rows_at(ref, start, size):
    return ref.at[pl.ds(pl.multiple_of(start, 16), size)]


def forward_kernel(
    rows_n, x_in, w_in, b_in, seg_wide, seg_row, x_turned, qkv, lse, mixed, *scratch
):
    x_all, blend, lse_cols, x_send, x_recv, o_send, o_recv, own_sem = scratch
    place = Place()
    me = place.pos
    mate, across = flip(me, 1), flip(me, 2)
    far = flip(mate, 2)
    peers = [mate, across, far]
    part = x_in.shape[0] // rows_n
    length = 4 * part
    width = w_in.shape[1] // 3
    heads = width // HEAD_DIM
    greet([(place.row, peer) for peer in peers])
    x_sems, o_sems = (x_send, x_recv), (o_send, o_recv)

    def x_spot(r, owner):
        return rows_at(x_all, r * length + owner * part, part)

    to_across, to_mate, passed, own = [], [], [], []
    for r in range(rows_n):
        src = x_in.at[pl.ds(r * part, part)]
        to_across.append(remote(src, x_spot(r, me), x_sems, (0, r), (place.row, across)))
        to_mate.append(remote(src, x_spot(r, me), x_sems, (1, r), (place.row, mate)))
        passed.append(
            remote(x_spot(r, across), x_spot(r, across), x_sems, (2, r), (place.row, mate))
        )
        own.append(pltpu.make_async_copy(src, x_spot(r, me), own_sem.at[r]))
        to_across[r].start()
        to_mate[r].start()
        own[r].start()
    is_query = lax.broadcasted_iota(jnp.int32, (1, 3 * width), 1) < width
    scale = jnp.where(is_query, SCALE, 1.0)
    out_copies = []
    for r in range(rows_n):
        to_across[r].wait_recv()
        passed[r].start()
        to_mate[r].wait_recv()
        own[r].wait()
        passed[r].wait_recv()
        base = r * length
        x_row = x_all[base : base + length, :]
        made = ((dot(x_row, w_in[...]) + b_in[...]) * scale).astype(LOW)
        for index in range(3 * heads):
            qkv[index, base : base + length, :] = made[:, index * HEAD_DIM : (index + 1) * HEAD_DIM]

        @pl.loop(0, length // LANES)
        def _(block):
            here = pl.ds(pl.multiple_of(base + block * LANES, LANES), LANES)
            local = pl.ds(pl.multiple_of(block * LANES, LANES), LANES)
            seg_q = seg_wide[r, local, :]
            same = jnp.concatenate([seg_q] * (length // LANES), axis=1) == seg_row[r : r + 1, :]
            for head in range(heads):
                query = qkv[head, here, :]
                key = qkv[heads + head, base : base + length, :]
                value = qkv[2 * heads + head, base : base + length, :]
                scores = jnp.where(same, dot_nt(query, key), MASKED)
                top = jnp.max(scores, axis=-1, keepdims=True)
                power = jnp.exp(scores - top)
                total = jnp.sum(power, axis=-1, keepdims=True)
                out = dot(power.astype(LOW), value) / total
                blend[here, head * HEAD_DIM : (head + 1) * HEAD_DIM] = out.astype(LOW)
                column = r * heads + head
                lse_cols[local, column : column + 1] = top + jnp.log(total)

        for index, peer in enumerate(peers):
            copy = remote(
                rows_at(blend, base + peer * part, part),
                mixed.at[me, pl.ds(r * part, part)],
                o_sems,
                (index, r),
                (place.row, peer),
            )
            copy.start()
            out_copies.append(copy)
        mixed[me, r * part : (r + 1) * part, :] = blend[
            pl.ds(pl.multiple_of(base + me * part, 16), part), :
        ]
    lse[...] = jnp.transpose(lse_cols[...])[: lse.shape[0], :]
    half = x_turned.shape[0]
    for r in range(rows_n):
        base = r * length
        block = x_all[base : base + length, pl.ds(pl.multiple_of(bit_of(me, 1) * half, LANES), half)]
        x_turned[:, base : base + length] = jnp.transpose(block)
    for copy in to_across + to_mate + passed:
        copy.wait_send()
    for copy in out_copies:
        copy.wait()


def attend_forward(x_rows, w_own, b_own, seg_wide, seg_row, rows_n):
    tokens_n, features = x_rows.shape
    length = seg_row.shape[1]
    every = rows_n * length
    width = w_own.shape[1] // 3
    vmem = pl.BlockSpec(memory_space=pltpu.VMEM)
    dma = pltpu.SemaphoreType.DMA
    return pl.pallas_call(
        partial(forward_kernel, rows_n),
        out_shape=[
            jax.ShapeDtypeStruct((features // 2, every), LOW),
            jax.ShapeDtypeStruct((3 * width // HEAD_DIM, every, HEAD_DIM), LOW),
            jax.ShapeDtypeStruct((16, length), F32),
            jax.ShapeDtypeStruct((4, tokens_n, width), LOW),
        ],
        in_specs=[vmem] * 5,
        out_specs=[vmem] * 4,
        scratch_shapes=[
            pltpu.VMEM((every, features), LOW),
            pltpu.VMEM((every, width), LOW),
            pltpu.VMEM((length, LANES), F32),
            dma((3, rows_n)),
            dma((3, rows_n)),
            dma((3, rows_n)),
            dma((3, rows_n)),
            dma((rows_n,)),
        ],
        compiler_params=pltpu.CompilerParams(
            collective_id=1, has_side_effects=True, vmem_limit_bytes=VMEM_LIMIT
        ),
        cost_estimate=pl.CostEstimate(
            flops=10**10, bytes_accessed=10**7, transcendentals=4 * 10**6
        ),
        name="attend_forward",
    )(x_rows, w_own, b_own, seg_wide, seg_row)


def plan_splits(rows, cols, links):
    kinds = []
    for _ in links:
        if (rows // 2) % 16 == 0:
            rows //= 2
            kinds.append("rows")
        elif (cols // 2) % LANES == 0:
            cols //= 2
            kinds.append("cols")
        else:
            kinds.append("whole")
    return kinds


def shrink(rows, cols, kind):
    return (rows // 2 if kind == "rows" else rows, cols // 2 if kind == "cols" else cols)


def landing_shape(rows, cols, links):
    total, widest = 0, 0
    for kind in plan_splits(rows, cols, links):
        rows, cols = shrink(rows, cols, kind)
        total, widest = total + rows, max(widest, cols)
    return total, widest


def add_into(dst, left, right, rows):
    step = 16 if rows % 48 else 48

    @pl.loop(0, rows // step)
    def _(i):
        at = pl.ds(pl.multiple_of(i * step, step), step)
        dst[at, :] = (left[at, :].astype(F32) + right[at, :].astype(F32)).astype(dst.dtype)


def window(ref, row0, rows, col0, cols):
    if not isinstance(row0, int):
        row0 = pl.multiple_of(row0, 16)
    if not isinstance(col0, int):
        col0 = pl.multiple_of(col0, LANES)
    return ref.at[pl.ds(row0, rows), pl.ds(col0, cols)]


class Chunk:
    def __init__(self, place, fixed, path, gather, give, out, total, landing, sems):
        send_sem, recv_sem, copy_sem = sems
        self.reduces, self.gathers, self.moment, self.gave = [], [], 0, False
        rows, cols = out.shape
        row0, col0, landed, slot = 0, 0, 0, 0
        corner = None
        row_trail, col_trail, kind_of = [], [], {}

        def held(at, rows, cols):
            return window(total, at[0] - corner[0], rows, at[1] - corner[1], cols)

        shape = out.shape
        for _, kind in fixed:
            shape = shrink(*shape, kind)
        kinds = [kind for _, kind in fixed] + plan_splits(*shape, path)
        for number, (link, kind) in enumerate(zip([link for link, _ in fixed] + path, kinds)):
            side = place.side(link)
            kind_of[link] = kind
            keep = other = (row0, col0)
            if kind == "rows":
                row_trail.append((row0, rows))
                rows //= 2
                keep, other = (row0 + side * rows, col0), (row0 + (1 - side) * rows, col0)
            elif kind == "cols":
                col_trail.append((col0, cols))
                cols //= 2
                keep, other = (row0, col0 + side * cols), (row0, col0 + (1 - side) * cols)
            row0, col0 = keep
            if number == max(len(fixed) - 1, 0):
                corner = keep
            if number < len(fixed):
                continue
            land = window(landing, landed, rows, 0, cols)
            landed += rows
            src = give if number == 0 else held(other, rows, cols)
            copy = remote(src, land, (send_sem, recv_sem), slot, place.partner(link))
            slot += 1
            self.reduces.append((copy, held(keep, rows, cols), land, kind == "whole"))
        mine = window(out, row0, rows, col0, cols)
        self.own = pltpu.make_async_copy(held((row0, col0), rows, cols), mine, copy_sem)
        for link in gather:
            kind = kind_of[link]
            if kind == "whole":
                self.gathers.append(None)
                continue
            here = window(out, row0, rows, col0, cols)
            self.gathers.append(remote(here, here, (send_sem, recv_sem), slot, place.partner(link)))
            slot += 1
            if kind == "rows":
                row0, rows = row_trail.pop()
            else:
                col0, cols = col_trail.pop()

    def done(self):
        return self.moment > len(self.reduces) + len(self.gathers)

    def advance(self):
        count, now = len(self.reduces), self.moment
        if 0 < now <= count:
            copy, keep, land, whole = self.reduces[now - 1]
            copy.wait_recv()
            if whole:
                copy.wait_send()
            add_into(keep, keep, land, land.shape[0])
        elif now > count and self.gathers[now - count - 1] is not None:
            self.gathers[now - count - 1].wait_recv()
        if now < count:
            self.reduces[now][0].start()
        elif now < count + len(self.gathers):
            if now == count:
                self.own.start()
                self.own.wait()
            if self.gathers[now - count] is not None:
                self.gathers[now - count].start()
        else:
            for index, (copy, _, _, whole) in enumerate(self.reduces):
                if not whole and not (index == 0 and self.gave):
                    copy.wait_send()
            for copy in self.gathers:
                if copy is not None:
                    copy.wait_send()
        self.moment += 1


PATHS = ("cxyzw", "cyxzw", "czwxy", "cyxzw", "cxyzw", "czwxy", "cxyzw", "czwxy", "cyzwx")
LATE_PATHS = ("wzxyc", "wzyxc", "wzyxc")
TICKS = (
    (),
    (),
    (),
    (),
    (0, 1, 2, 3),
    (),
    (),
    (4,),
    (),
    (0, 1, 2, 5),
    (6,),
    (3,),
    (0, 1, 4, 7),
    (0, 2, 5, 6, 1),
    (3,),
    (8, 0, 2, 4, 7),
    (),
    (6,),
    (5, 3),
    (1,),
    (0, 4, 8, 2),
    (5, 6),
    (),
    (),
    (0, 2, 3, 7, 1, 5),
    (),
    (4, 8),
    (6,),
    (1, 2, 3),
)
DRAIN = (7, 4, 9, 8, 10, 6, 3, 11, 4, 9, 0, 1, 5, 10, 8, 2, 7, 6, 11, 3, 4, 9, 10, 11, 0, 1, 7, 2, 5, 9, 8, 10, 0, 6, 1, 2, 11, 4, 9, 7, 3, 4, 5, 10, 3, 11, 8, 6, 9, 6, 10, 7, 11, 5, 8, 5, 9, 10, 9, 7, 10, 11, 7, 8, 11, 8)
TAIL_STEEP = 0.24
TAIL = (
    0.09575598852910579,
    0.09547705164870551,
    0.093198719112773,
    0.06193635630868121,
    0.1216760657292812,
    -0.06984360139735674,
    0.1555215658230106,
    -0.05372215169653546,
)
TILE = 256
BAND = 48
SLOTS = 4


def gelu_and_slope(u):
    bell = jnp.exp(u * u * -0.5)
    t = 1.0 / (1.0 + TAIL_STEEP * jnp.abs(u))
    f = TAIL[-1]
    for coefficient in TAIL[-2::-1]:
        f = f * t + coefficient
    below = f * t * bell
    phi = jnp.where(u > 0, 1.0 - below, below)
    return u * phi, phi + u * (bell * 0.3989422804014327)


def fold(v):
    return jnp.sum(v.reshape(v.shape[0] // 8, 8, v.shape[1]), axis=0)


def bands(n, init, body):
    def step(i, carry):
        return body(pl.ds(pl.multiple_of(i * BAND, BAND), BAND), carry)

    return lax.fori_loop(0, n // BAND, step, init)


def rest_kernel(rows_n, paths, late_paths, links, *refs):
    (x_in, mixed, cot, vecs, up_bias, lse, seg_wide, seg_row) = refs[:8]
    (qkv_in, turned_in, w_out_in, w_up_in, w_down_in, w_own_in, w_mate_in) = refs[8:15]
    (q_out, k_out, v_out, o_out, up_out, down_out, result, dx_out, small_out) = refs[15:24]
    (d_give, d_all, chip, dx_give, dx_land, gives, total, late_total, landing, late_land) = refs[24:34]
    (small_land, send_sem, recv_sem, copy_sem, small_send, small_recv) = refs[34:40]
    (d_send, d_recv, g_send, g_recv, dx_send, dx_recv, load_sem) = refs[40:47]
    place = Place()
    me = place.pos
    mate, across = flip(me, 1), flip(me, 2)
    peers = [across, flip(mate, 2), mate]
    core = bit_of(me, 1)
    tokens_n, features = x_in.shape
    part = tokens_n // rows_n
    length = 4 * part
    width = d_all.shape[1]
    heads = width // HEAD_DIM
    inner_n = up_bias.shape[1]
    half = features // 2
    quarters = inner_n // features
    outs = [window(down_out, j * features, features, 0, features) for j in range(inner_n // features)]
    outs += [window(up_out, 0, features, j * features, features) for j in range(inner_n // features)]
    outs += [o_out]
    chunks = []
    for index, out in enumerate(outs + [q_out, k_out, v_out]):
        sems = (send_sem.at[index], recv_sem.at[index], copy_sem.at[index])
        if index < len(outs):
            path = paths[index]
            spaces = (gives.at[index % SLOTS], out, total.at[index], landing.at[index])
            chunks.append(Chunk(place, [], path, path[::-1], *spaces, sems))
        else:
            at = index - len(outs)
            fixed = [(links[0], "rows"), (links[1], "cols")]
            spaces = (None, out, late_total.at[at], late_land.at[at])
            chunks.append(Chunk(place, fixed, links[2:], late_paths[at], *spaces, sems))
    mine, other = chip.at[core], chip.at[1 - core]
    d_copies, g_copies, dx_copies = {}, [], []
    for r in range(rows_n):
        at = pl.ds(r * part, part)
        row = pl.ds(r * length, length)
        for index, peer in enumerate(peers):
            d_copies[index, r] = remote(
                d_give.at[peer, at],
                rows_at(d_all, r * length + me * part, part),
                (d_send, d_recv),
                (index, r),
                (place.row, peer),
            )
        g_copies.append(
            remote(mine.at[row], mine.at[row], (g_send, g_recv), r, (place.row, mate))
        )
        dx_copies.append(
            remote(dx_give.at[at], dx_land.at[at], (dx_send, dx_recv), r, (place.row, across))
        )
    ticks = [0]

    def tick():
        for index in TICKS[ticks[0]]:
            if chunks[index].moment > 0 and not chunks[index].done():
                chunks[index].advance()
        ticks[0] += 1

    def new_chunk(index, give, keep):
        chunk = chunks[index]
        if index >= SLOTS:
            chunks[index - SLOTS].reduces[0][0].wait_send()
            chunks[index - SLOTS].gave = True
        gives[index % SLOTS] = give().astype(LOW)
        chunk.advance()
        total[index] = keep().astype(LOW)

    greet([place.partner(link) for link in links] + [(place.row, flip(mate, 2))])
    give_at = pl.ds(pl.multiple_of((1 - core) * half, LANES), half)
    keep_at = pl.ds(pl.multiple_of(core * half, LANES), half)
    small_out[...] = jnp.zeros_like(small_out)

    def dense(w_out, w_up, w_down, joined, hat, spread_one, low, turned, active, slope, d_low, d_up):
        acc = dx_out
        loads = []
        for index, (src, dst) in enumerate(((w_out_in, w_out), (w_up_in, w_up), (w_down_in, w_down))):
            loads.append(pltpu.make_async_copy(src, dst, load_sem.at[index]))
            loads[-1].start()
        for group in range(4):
            joined[:, group * width : (group + 1) * width] = mixed[group]
        gain_one, shift_one = vecs[1:2, :], vecs[2:3, :]
        gain_two, shift_two = vecs[4:5, :], vecs[5:6, :]
        loads[0].wait()
        acc[...] = dot(joined[...], w_out[...])

        def norm_one(at, carry):
            v = x_in[at, :].astype(F32) + (acc[at, :] + vecs[0:1, :])
            centred = v - jnp.mean(v, axis=-1, keepdims=True)
            over = lax.rsqrt(jnp.mean(centred * centred, axis=-1, keepdims=True) + EPS)
            v = centred * over
            hat[at, :] = v
            spread_one[at, :] = jnp.broadcast_to(over, (BAND, LANES))
            low[at, :] = (v * gain_one + shift_one).astype(LOW)
            return carry

        bands(tokens_n, 0, norm_one)
        loads[1].wait()

        @pl.loop(0, inner_n // TILE)
        def _(tile):
            cols = pl.ds(pl.multiple_of(tile * TILE, TILE), TILE)
            u = dot(low[...], w_up[:, cols]) + up_bias[:, cols]
            for band in range(tokens_n // BAND):
                at = slice(band * BAND, (band + 1) * BAND)
                g, s = gelu_and_slope(u[at])
                active[at, cols] = g.astype(LOW)
                slope[at, cols] = s

        loads[2].wait()

        @pl.loop(0, features // TILE)
        def _(tile):
            cols = pl.ds(pl.multiple_of(tile * TILE, TILE), TILE)
            acc[:, cols] = dot(active[...], w_down[:, cols])

        def norm_two(at, carry):
            d_gain, d_shift, d_bias = carry
            v = hat[at, :] * gain_one + shift_one + (acc[at, :] + vecs[3:4, :])
            centred = v - jnp.mean(v, axis=-1, keepdims=True)
            over = lax.rsqrt(jnp.mean(centred * centred, axis=-1, keepdims=True) + EPS)
            v = centred * over
            result[at, :] = (v * gain_two + shift_two).astype(LOW)
            d = cot[at, :].astype(F32)
            d_gain += fold(d * v)
            d_shift += fold(d)
            d = d * gain_two
            d = d - jnp.mean(d, axis=-1, keepdims=True) - v * jnp.mean(d * v, axis=-1, keepdims=True)
            d = d * over
            acc[at, :] = d
            d = d.astype(LOW)
            d_low[at, :] = d
            return d_gain, d_shift, d_bias + fold(d.astype(F32))

        blank = jnp.zeros((8, features), F32)
        d_gain, d_shift, d_bias = bands(tokens_n, (blank, blank, blank), norm_two)
        for index, value in ((3, d_bias), (4, d_gain), (5, d_shift)):
            small_out[index : index + 1, :] = jnp.sum(value, axis=0, keepdims=True)

        for quarter in range(quarters):
            first = quarter * features

            def some_down(side):
                at = pl.ds(pl.multiple_of(first + side * half, LANES), half)
                return dot_tn(active[:, at], d_low[...])

            new_chunk(quarter, lambda: some_down(1 - core), lambda: some_down(core))
            tick()
        turned[...] = jnp.transpose(low[...])
        for quarter in range(quarters):
            first = quarter * features

            @pl.loop(0, features // TILE)
            def _(tile):
                rows = pl.ds(pl.multiple_of(first + tile * TILE, TILE), TILE)
                cols = pl.ds(pl.multiple_of(tile * TILE, TILE), TILE)
                d = (dot_nt(d_low[...], w_down[rows, :]) * slope[:, rows]).astype(LOW)
                d_up[:, cols] = d
                small_out[12 + quarter : 13 + quarter, cols] = jnp.sum(
                    d.astype(F32), axis=0, keepdims=True
                )

            tick()
            new_chunk(
                quarters + quarter,
                lambda: dot(turned[give_at, :], d_up[...]),
                lambda: dot(turned[keep_at, :], d_up[...]),
            )
            acc[...] += dot_nt(d_up[...], w_up[:, first : first + features])
            tick()

        def norm_back(at, carry):
            d_gain, d_shift, d_bias = carry
            v, d = hat[at, :], acc[at, :]
            d_gain += fold(d * v)
            d_shift += fold(d)
            d = d * gain_one
            d = d - jnp.mean(d, axis=-1, keepdims=True) - v * jnp.mean(d * v, axis=-1, keepdims=True)
            d = d * spread_one[at, 0:1]
            acc[at, :] = d
            d = d.astype(LOW)
            d_low[at, :] = d
            return d_gain, d_shift, d_bias + fold(d.astype(F32))

        d_gain, d_shift, d_bias = bands(tokens_n, (blank, blank, blank), norm_back)
        for index, value in ((0, d_bias), (1, d_gain), (2, d_shift)):
            small_out[index : index + 1, :] = jnp.sum(value, axis=0, keepdims=True)
        for group in range(4):
            at = slice(group * width, (group + 1) * width)
            d_give[group] = dot_nt(d_low[...], w_out[at, :]).astype(LOW)
        for r in range(rows_n):
            for index in range(3):
                d_copies[index, r].start()
        new_chunk(
            2 * quarters,
            lambda: dot_tn(joined[:, give_at], d_low[...]),
            lambda: dot_tn(joined[:, keep_at], d_low[...]),
        )
        tick()

    square = (tokens_n, features)
    pl.run_scoped(
        dense,
        pltpu.VMEM((features, features), LOW),
        pltpu.VMEM((features, inner_n), LOW),
        pltpu.VMEM((inner_n, features), LOW),
        pltpu.VMEM(square, LOW),
        pltpu.VMEM(square, F32),
        pltpu.VMEM((tokens_n, LANES), F32),
        pltpu.VMEM(square, LOW),
        pltpu.VMEM((features, tokens_n), LOW),
        pltpu.VMEM((tokens_n, inner_n), LOW),
        pltpu.VMEM((tokens_n, inner_n), F32),
        pltpu.VMEM(square, LOW),
        pltpu.VMEM(square, LOW),
    )

    def attention(qkv, x_turned, w_own, w_mate, d_heads, prob, d_score):
        loads = []
        for index, (src, dst) in enumerate(
            ((qkv_in, qkv), (turned_in, x_turned), (w_own_in, w_own), (w_mate_in, w_mate))
        ):
            loads.append(pltpu.make_async_copy(src, dst, load_sem.at[index]))
            loads[-1].start()
        for load in loads:
            load.wait()
        for r in range(rows_n):
            base = r * length
            own_rows = pl.ds(pl.multiple_of(base + me * part, 16), part)
            d_all[own_rows, :] = d_give[me, r * part : (r + 1) * part, :]
            for index in range(3):
                d_copies[index, r].wait_recv()
            d_row = d_all[base : base + length, :]
            for head in range(heads):
                d_heads[head] = d_row[:, head * HEAD_DIM : (head + 1) * HEAD_DIM]

            def scores(block):
                here = pl.ds(pl.multiple_of(base + block * LANES, LANES), LANES)
                local = pl.ds(pl.multiple_of(block * LANES, LANES), LANES)
                same = seg_wide[r] == seg_row[r : r + 1, local]
                for head in range(heads):
                    query = qkv[head, here, :]
                    key = qkv[heads + head, base : base + length, :]
                    value = qkv[2 * heads + head, base : base + length, :]
                    log_total = lse[r * heads + head : r * heads + head + 1, local]
                    p = jnp.exp(jnp.where(same, dot_nt(key, query) - log_total, MASKED))
                    dp = dot_nt(value, d_heads[head, local, :])
                    inner = jnp.sum(dp * p, axis=0, keepdims=True)
                    prob[head, :, local] = p.astype(LOW)
                    d_score[head, :, local] = (p * (dp - inner)).astype(LOW)

            blocks = length // LANES
            pl.loop(0, blocks // 2)(scores)
            tick()
            pl.loop(blocks // 2, blocks)(scores)
            tick()
            for head in range(heads):
                query = qkv[head, base : base + length, :]
                key = qkv[heads + head, base : base + length, :]
                ds = d_score[head]
                at = slice(base, base + length)
                left = head * HEAD_DIM
                dq = dot_tn(ds, key) * SCALE
                mine[at, left : left + HEAD_DIM] = dq.astype(LOW)
                left += width
                mine[at, left : left + HEAD_DIM] = dot(ds, query).astype(LOW)
                left += width
                mine[at, left : left + HEAD_DIM] = dot(prob[head], d_heads[head]).astype(LOW)
            g_copies[r].start()
            tick()

        def dx_of(r, owner):
            at = pl.ds(pl.multiple_of(r * length + owner * part, 16), part)
            return dot_nt(mine[at, :], w_own[...]) + dot_nt(other[at, :], w_mate[...])

        for r in range(rows_n):
            g_copies[r].wait_recv()
            at = pl.ds(r * part, part)
            dx_give[at, :] = dx_of(r, across).astype(LOW)
            dx_copies[r].start()
            tick()
        for index in range(3):
            left = index * width
            sums = [dot(x_turned[...], chip[side, :, left : left + width]) for side in range(2)]
            late_total[index] = jnp.concatenate(sums, axis=1).astype(LOW)
            chunks[2 * quarters + 1 + index].advance()
            tick()
        token_sums = jnp.sum(mine[...].astype(F32), axis=0, keepdims=True)
        group = lax.broadcasted_iota(jnp.int32, (4, 3 * width), 0)
        spread = jnp.where(group == me, token_sums, 0.0)
        spread = jnp.concatenate([spread, jnp.zeros((4, features - 3 * width), F32)], axis=1)
        small_out[8:12, :] = spread
        for r in range(rows_n):
            at = pl.ds(r * part, part)
            dx_out[at, :] += dx_of(r, me)
        tick()

    pl.run_scoped(
        attention,
        pltpu.VMEM(qkv_in.shape, LOW),
        pltpu.VMEM(turned_in.shape, LOW),
        pltpu.VMEM(w_own_in.shape, LOW),
        pltpu.VMEM(w_mate_in.shape, LOW),
        pltpu.VMEM((heads, length, HEAD_DIM), LOW),
        pltpu.VMEM((heads, length, length), LOW),
        pltpu.VMEM((heads, length, length), LOW),
    )
    smalls = [
        remote(
            small_out, small_land.at[number], (small_send, small_recv), number, place.partner(link)
        )
        for number, link in enumerate(links)
    ]
    gap = len(DRAIN) // (len(links) + 1)

    def small_step(number):
        if 0 < number <= len(links):
            smalls[number - 1].wait()
            small_out[...] += small_land[number - 1]
        if number < len(links):
            smalls[number].start()

    for at, index in enumerate(DRAIN):
        if at % gap == 0:
            small_step(at // gap)
        if not chunks[index].done():
            chunks[index].advance()
    for number in range((len(DRAIN) - 1) // gap + 1, len(links) + 1):
        small_step(number)
    while not all(chunk.done() for chunk in chunks):
        for chunk in chunks:
            if not chunk.done():
                chunk.advance()
    for r in range(rows_n):
        dx_copies[r].wait_recv()
        at = pl.ds(r * part, part)
        dx_out[at, :] += dx_land[at, :].astype(F32)
    for copy in dx_copies + g_copies + list(d_copies.values()):
        copy.wait_send()


def attend_rest(mesh_shape, x_rows, mixed, cot, vecs, up_bias, lse, seg_wide, seg_row, qkv, x_turned, w_out, w_up, w_down, w_own, w_mate):
    row_bits = [("r", bit) for bit in axis_bits(mesh_shape["rows"])]
    pos_bits = [("p", bit) for bit in axis_bits(mesh_shape["pos"])]
    name = dict(zip("cyxzw", pos_bits + row_bits))
    paths = [[name[letter] for letter in path] + row_bits[3:] for path in PATHS]
    late_paths = [row_bits[3:][::-1] + [name[letter] for letter in path] for path in LATE_PATHS]
    links = pos_bits + row_bits
    rows_n, length = seg_row.shape
    tokens_n, features = x_rows.shape
    inner_n = w_up.shape[1]
    width = mixed.shape[2]
    every = rows_n * length
    steps = len(links)
    half = features // 2
    early = landing_shape(features, features, links)
    late = landing_shape(half, half, row_bits)
    vmem = pl.BlockSpec(memory_space=pltpu.VMEM)
    hbm = pl.BlockSpec(memory_space=pl.ANY)
    dma = pltpu.SemaphoreType.DMA
    square = jax.ShapeDtypeStruct((features, features), LOW)
    return pl.pallas_call(
        partial(rest_kernel, rows_n, paths, late_paths, links),
        out_shape=[
            square,
            square,
            square,
            square,
            jax.ShapeDtypeStruct(w_up.shape, LOW),
            jax.ShapeDtypeStruct(w_down.shape, LOW),
            jax.ShapeDtypeStruct((tokens_n, features), LOW),
            jax.ShapeDtypeStruct((tokens_n, features), F32),
            jax.ShapeDtypeStruct((16, features), F32),
        ],
        in_specs=[vmem] * 8 + [hbm] * 7,
        out_specs=[hbm] * 6 + [vmem] * 3,
        scratch_shapes=[
            pltpu.VMEM((4, tokens_n, width), LOW),
            pltpu.VMEM((every, width), LOW),
            pltpu.VMEM((2, every, 3 * width), LOW),
            pltpu.VMEM((tokens_n, features), LOW),
            pltpu.VMEM((tokens_n, features), LOW),
            pltpu.VMEM((SLOTS, half, features), LOW),
            pltpu.VMEM((9, half, features), LOW),
            pltpu.VMEM((3, half, half), LOW),
            pltpu.VMEM((9, *early), LOW),
            pltpu.VMEM((3, *late), LOW),
            pltpu.VMEM((steps, 16, features), F32),
            dma((12, 2 * steps)),
            dma((12, 2 * steps)),
            dma((12,)),
            dma((steps,)),
            dma((steps,)),
            dma((3, rows_n)),
            dma((3, rows_n)),
            dma((rows_n,)),
            dma((rows_n,)),
            dma((rows_n,)),
            dma((rows_n,)),
            dma((4,)),
        ],
        compiler_params=pltpu.CompilerParams(
            collective_id=0, has_side_effects=True, vmem_limit_bytes=VMEM_LIMIT
        ),
        cost_estimate=pl.CostEstimate(
            flops=4 * 10**10, bytes_accessed=8 * 10**7, transcendentals=8 * 10**6
        ),
        name="attend_rest",
    )(x_rows, mixed, cot, vecs, up_bias, lse, seg_wide, seg_row, qkv, x_turned, w_out, w_up, w_down, w_own, w_mate)


def widen_kernel(*refs):
    half = len(refs) // 2
    for src, dst in zip(refs[:half], refs[half:]):
        dst[...] = src[...].astype(F32)


def widen(arrays, steps):
    specs = [pl.BlockSpec((a.shape[0] // steps, a.shape[1]), lambda i: (i, 0)) for a in arrays]
    moved = sum(6 * a.size for a in arrays)
    return pl.pallas_call(
        widen_kernel,
        grid=(steps,),
        out_shape=[jax.ShapeDtypeStruct(a.shape, F32) for a in arrays],
        in_specs=specs,
        out_specs=specs,
        compiler_params=pltpu.CompilerParams(vmem_limit_bytes=VMEM_LIMIT),
        cost_estimate=pl.CostEstimate(flops=0, bytes_accessed=moved, transcendentals=0),
        name="widen",
    )(*arrays)


def own_columns(w, index, width):
    return lax.dynamic_slice_in_dim(w, index * width, width, w.ndim - 1)


def on_device(
    mesh_shape,
    tokens,
    segments,
    w_query,
    b_query,
    w_key,
    w_value,
    b_value,
    w_out,
    b_out,
    gain_one,
    shift_one,
    w_up,
    b_up,
    w_down,
    b_down,
    gain_two,
    shift_two,
    cotangent,
):
    rows_n, part_len, features = tokens.shape
    length = segments.shape[1]
    groups = mesh_shape["pos"]
    width = features // groups
    here = lax.axis_index("pos")
    mate = here + 1 - 2 * lax.rem(here, 2)
    x_rows = tokens.reshape(rows_n * part_len, features)
    seg_row = segments.astype(F32)
    seg_wide = jnp.broadcast_to(seg_row[:, :, None], (rows_n, length, LANES))

    def heads_of(index):
        return jnp.concatenate(
            [own_columns(w, index, width) for w in (w_query, w_key, w_value)], axis=1
        )

    w_own, w_mate = heads_of(here), heads_of(mate)
    b_own = jnp.concatenate(
        [
            own_columns(b_query.astype(F32), here, width),
            jnp.zeros((width,), F32),
            own_columns(b_value.astype(F32), here, width),
        ]
    )[None]
    x_turned, qkv, lse, mixed = attend_forward(x_rows, w_own, b_own, seg_wide, seg_row, rows_n)
    vecs = jnp.stack([b_out, gain_one, shift_one, b_down, gain_two, shift_two]).astype(F32)
    *blocks, result, grad_tokens, small = attend_rest(
        mesh_shape,
        x_rows,
        mixed,
        cotangent.reshape(rows_n * part_len, features),
        jnp.pad(vecs, ((0, 2), (0, 0))),
        b_up.astype(F32)[None],
        lse,
        seg_wide,
        seg_row,
        qkv,
        x_turned,
        w_out,
        w_up,
        w_down,
        w_own,
        w_mate,
    )
    grad_w_query, grad_w_key, grad_w_value, grad_w_out, grad_w_up, grad_w_down = widen(blocks, 12)
    shape = (rows_n, part_len, features)
    return (
        result.reshape(shape),
        grad_tokens.reshape(shape),
        grad_w_query,
        small[8:12, :width].reshape(-1),
        grad_w_key,
        grad_w_value,
        small[8:12, 2 * width : 3 * width].reshape(-1),
        grad_w_out,
        small[0],
        small[1],
        small[2],
        grad_w_up,
        small[12:16].reshape(-1),
        grad_w_down,
        small[3],
        small[4],
        small[5],
    )


def solution(mesh):
    tokens = P("rows", "pos", None)
    return jax.shard_map(
        partial(on_device, dict(mesh.shape)),
        mesh=mesh,
        in_specs=(tokens, P("rows", None), *[P()] * 15, tokens),
        out_specs=(tokens, tokens, *[P()] * 15),
        check_vma=False,
    )
```

profile of v0, /device:TPU:0, one launch (start us, length us, event | category | flops | bytes accessed | tf_op | source)
XLA Modules:
  0.0 238.5 jit_solution(9223391743198474272)
XLA Ops:
  0.7 0.0 copy-start.2
  0.7 0.0 copy-start.3
  0.7 0.9 dynamic_slice.27
  1.6 0.8 dynamic_slice.28
  2.4 0.1 pad_maximum_fusion.2
  2.4 0.6 broadcast_in_dim.18.b_in
  3.0 0.7 stack.21
  3.7 0.7 stack.22
  4.4 0.7 stack.23
  5.1 0.7 stack.24
  5.8 0.7 stack.25
  6.4 0.7 stack.26
  7.2 0.7 convert_element_type.15.seg_row.refs_7_
  7.9 0.0 copy-start.4
  7.9 0.6 pad_convert_fusion.refs_3_
  8.5 1.3 broadcast_in_dim.22
  9.8 1.6 constant_dynamic-slice_fusion.2
  11.4 1.3 broadcast_in_dim.19.seg_wide.refs_6_
  12.7 0.0 copy-done.2
  12.7 0.0 copy-done.3
  12.7 0.8 constant_dynamic-slice_fusion
  13.4 0.0 copy-done.4
  13.4 1.3 pad_maximum_fusion.1.refs_14_
  14.7 1.3 pad_maximum_fusion.w_in.refs_13_
  16.0 43.7 %attend_forward.1 = (bf16[384,1920]{1,0:T(8,128)(2,1)}, bf16[9,1920,64]{2,1,0:T(8,128)(2,1)}, f32[16,640]{1,0:T(8,128)}, bf16[4,480,192]{2,1,0:T(8,128)(2,1)}) custom-call(bf16[480,768]{1,0:T(8,128)(2,1)} %bitcast.8, bf16[768,576]{1,0:T(8,128)(2,1)} %pad_maximum_fusion.w_in.refs_13_, f32[1,576]{1,0:T(1,128)} %broadcast_in_dim.18.b_in, ...), custom_call_target="tpu_custom_call" | custom-call | flops 10000000000 | bytes 10000000 | tf_op jit(solution)/shard_map/attend_forward/pallas_call | solution.py:183
  59.8 154.7 %attend_rest.1 = (bf16[768,768]{1,0:T(8,128)(2,1)}, bf16[768,768]{1,0:T(8,128)(2,1)}, bf16[768,768]{1,0:T(8,128)(2,1)}, bf16[768,768]{1,0:T(8,128)(2,1)}, bf16[7...) custom-call(bf16[480,768]{1,0:T(8,128)(2,1)} %bitcast.9, ...), custom_call_target="tpu_custom_call" | custom-call | flops 40000000000 | bytes 80000000 | tf_op jit(solution)/shard_map/attend_rest/pallas_call | solution.py:777
  214.5 0.7 fusion
  215.2 0.7 reshape.61
  215.9 0.7 reshape.60
  216.5 0.7 slice.32
  217.3 1.7 slice_reduce_fusion
  219.0 0.6 reshape.62
  219.6 0.0 copy-start.1
  219.6 15.7 %widen.1 = (f32[768,768]{1,0:T(8,128)}, f32[768,768]{1,0:T(8,128)}, f32[768,768]{1,0:T(8,128)}, f32[768,768]{1,0:T(8,128)}, f32[768,3072]{1,0:T(8,128)}, /*index=5*/f32[3072,768]{1,0:T(8,128)}) custom-call(bf16[768,768]{1,0:T(8,128)(2,1)} %get-tuple-element.42.refs_0_, bf16[768,768]{1,0:T(8,128)(2,1)} %get-tuple-element.43.refs_1_, ...), custom_call_target="tpu_custom_call" | custom-call | bytes 42467328 | tf_op jit(solution)/shard_map/widen/pallas_call | solution.py:836
  235.3 0.0 copy-start
  235.3 0.0 copy-done.1
  235.3 0.9 copy.37
  236.2 0.8 copy-done
  237.0 1.1 copy.38
  (2 shorter events, 0.0 us)
Async XLA Ops:
  0.7 12.0 %copy-start.2 = (bf16[768,768]{1,0:T(8,128)(2,1)S(1)}, bf16[768,768]{1,0:T(8,128)(2,1)}, u32[]{:S(2)}) copy-start(bf16[768,768]{1,0:T(8,128)(2,1)} %param.23) | copy-start | bytes 3538948
  0.7 12.0 %copy-start.3 = (bf16[768,768]{1,0:T(8,128)(2,1)S(1)}, bf16[768,768]{1,0:T(8,128)(2,1)}, u32[]{:S(2)}) copy-start(bf16[768,768]{1,0:T(8,128)(2,1)} %param.22) | copy-start | bytes 3538948
  7.9 5.6 %copy-start.4 = (f32[3,640]{1,0:T(4,128)}, f32[3,640]{1,0:T(4,128)S(1)}, u32[]{:S(2)}) copy-start(f32[3,640]{1,0:T(4,128)S(1)} %convert_element_type.15.seg_row.refs_7_) | copy-start | bytes 23044
  219.6 15.7 %copy-start.1 = (bf16[480,768]{1,0:T(8,128)(2,1)S(1)}, bf16[480,768]{1,0:T(8,128)(2,1)}, u32[]{:S(2)}) copy-start(bf16[480,768]{1,0:T(8,128)(2,1)} %get-tuple-element.40) | copy-start | bytes 2211844
  235.3 1.6 copy-start
where the time goes:
time: 242 us; the launch traced here: 239 us
  Pallas kernels  214 us (88%)
  local copies, waits for them, and re-layouts  17.9 us (7%)
  other arithmetic  5.28 us (2%)
    pallas_call x1, Pallas kernels, attend_rest(): pl.pallas_call(partial(rest_kernel, rows_n, paths, late_paths, links), ou...  155 us
    pallas_call x1, Pallas kernels, attend_forward(): pl.pallas_call(partial(forward_kernel, rows_n), out_shape=[jax.ShapeDtype...  43.7 us
    pallas_call x1, Pallas kernels, widen(): pl.pallas_call(widen_kernel, grid=(steps,), out_shape=[jax.ShapeDtypeStru...  15.7 us

commit v1 on v0

--- a/solution.py
+++ b/solution.py
@@ -81,133 +81,6 @@
 
 def rows_at(ref, start, size):
     return ref.at[pl.ds(pl.multiple_of(start, 16), size)]
-
-
-def forward_kernel(
-    rows_n, x_in, w_in, b_in, seg_wide, seg_row, x_turned, qkv, lse, mixed, *scratch
-):
-    x_all, blend, lse_cols, x_send, x_recv, o_send, o_recv, own_sem = scratch
-    place = Place()
-    me = place.pos
-    mate, across = flip(me, 1), flip(me, 2)
-    far = flip(mate, 2)
-    peers = [mate, across, far]
-    part = x_in.shape[0] // rows_n
-    length = 4 * part
-    width = w_in.shape[1] // 3
-    heads = width // HEAD_DIM
-    greet([(place.row, peer) for peer in peers])
-    x_sems, o_sems = (x_send, x_recv), (o_send, o_recv)
-
-    def x_spot(r, owner):
-        return rows_at(x_all, r * length + owner * part, part)
-
-    to_across, to_mate, passed, own = [], [], [], []
-    for r in range(rows_n):
-        src = x_in.at[pl.ds(r * part, part)]
-        to_across.append(remote(src, x_spot(r, me), x_sems, (0, r), (place.row, across)))
-        to_mate.append(remote(src, x_spot(r, me), x_sems, (1, r), (place.row, mate)))
-        passed.append(
-            remote(x_spot(r, across), x_spot(r, across), x_sems, (2, r), (place.row, mate))
-        )
-        own.append(pltpu.make_async_copy(src, x_spot(r, me), own_sem.at[r]))
-        to_across[r].start()
-        to_mate[r].start()
-        own[r].start()
-    is_query = lax.broadcasted_iota(jnp.int32, (1, 3 * width), 1) < width
-    scale = jnp.where(is_query, SCALE, 1.0)
-    out_copies = []
-    for r in range(rows_n):
-        to_across[r].wait_recv()
-        passed[r].start()
-        to_mate[r].wait_recv()
-        own[r].wait()
-        passed[r].wait_recv()
-        base = r * length
-        x_row = x_all[base : base + length, :]
-        made = ((dot(x_row, w_in[...]) + b_in[...]) * scale).astype(LOW)
-        for index in range(3 * heads):
-            qkv[index, base : base + length, :] = made[:, index * HEAD_DIM : (index + 1) * HEAD_DIM]
-
-        @pl.loop(0, length // LANES)
-        def _(block):
-            here = pl.ds(pl.multiple_of(base + block * LANES, LANES), LANES)
-            local = pl.ds(pl.multiple_of(block * LANES, LANES), LANES)
-            seg_q = seg_wide[r, local, :]
-            same = jnp.concatenate([seg_q] * (length // LANES), axis=1) == seg_row[r : r + 1, :]
-            for head in range(heads):
-                query = qkv[head, here, :]
-                key = qkv[heads + head, base : base + length, :]
-                value = qkv[2 * heads + head, base : base + length, :]
-                scores = jnp.where(same, dot_nt(query, key), MASKED)
-                top = jnp.max(scores, axis=-1, keepdims=True)
-                power = jnp.exp(scores - top)
-                total = jnp.sum(power, axis=-1, keepdims=True)
-                out = dot(power.astype(LOW), value) / total
-                blend[here, head * HEAD_DIM : (head + 1) * HEAD_DIM] = out.astype(LOW)
-                column = r * heads + head
-                lse_cols[local, column : column + 1] = top + jnp.log(total)
-
-        for index, peer in enumerate(peers):
-            copy = remote(
-                rows_at(blend, base + peer * part, part),
-                mixed.at[me, pl.ds(r * part, part)],
-                o_sems,
-                (index, r),
-                (place.row, peer),
-            )
-            copy.start()
-            out_copies.append(copy)
-        mixed[me, r * part : (r + 1) * part, :] = blend[
-            pl.ds(pl.multiple_of(base + me * part, 16), part), :
-        ]
-    lse[...] = jnp.transpose(lse_cols[...])[: lse.shape[0], :]
-    half = x_turned.shape[0]
-    for r in range(rows_n):
-        base = r * length
-        block = x_all[base : base + length, pl.ds(pl.multiple_of(bit_of(me, 1) * half, LANES), half)]
-        x_turned[:, base : base + length] = jnp.transpose(block)
-    for copy in to_across + to_mate + passed:
-        copy.wait_send()
-    for copy in out_copies:
-        copy.wait()
-
-
-def attend_forward(x_rows, w_own, b_own, seg_wide, seg_row, rows_n):
-    tokens_n, features = x_rows.shape
-    length = seg_row.shape[1]
-    every = rows_n * length
-    width = w_own.shape[1] // 3
-    vmem = pl.BlockSpec(memory_space=pltpu.VMEM)
-    dma = pltpu.SemaphoreType.DMA
-    return pl.pallas_call(
-        partial(forward_kernel, rows_n),
-        out_shape=[
-            jax.ShapeDtypeStruct((features // 2, every), LOW),
-            jax.ShapeDtypeStruct((3 * width // HEAD_DIM, every, HEAD_DIM), LOW),
-            jax.ShapeDtypeStruct((16, length), F32),
-            jax.ShapeDtypeStruct((4, tokens_n, width), LOW),
-        ],
-        in_specs=[vmem] * 5,
-        out_specs=[vmem] * 4,
-        scratch_shapes=[
-            pltpu.VMEM((every, features), LOW),
-            pltpu.VMEM((every, width), LOW),
-            pltpu.VMEM((length, LANES), F32),
-            dma((3, rows_n)),
-            dma((3, rows_n)),
-            dma((3, rows_n)),
-            dma((3, rows_n)),
-            dma((rows_n,)),
-        ],
-        compiler_params=pltpu.CompilerParams(
-            collective_id=1, has_side_effects=True, vmem_limit_bytes=VMEM_LIMIT
-        ),
-        cost_estimate=pl.CostEstimate(
-            flops=10**10, bytes_accessed=10**7, transcendentals=4 * 10**6
-        ),
-        name="attend_forward",
-    )(x_rows, w_own, b_own, seg_wide, seg_row)
 
 
 def plan_splits(rows, cols, links):
@@ -410,24 +283,30 @@
     return lax.fori_loop(0, n // BAND, step, init)
 
 
-def rest_kernel(rows_n, paths, late_paths, links, *refs):
-    (x_in, mixed, cot, vecs, up_bias, lse, seg_wide, seg_row) = refs[:8]
-    (qkv_in, turned_in, w_out_in, w_up_in, w_down_in, w_own_in, w_mate_in) = refs[8:15]
-    (q_out, k_out, v_out, o_out, up_out, down_out, result, dx_out, small_out) = refs[15:24]
-    (d_give, d_all, chip, dx_give, dx_land, gives, total, late_total, landing, late_land) = refs[24:34]
-    (small_land, send_sem, recv_sem, copy_sem, small_send, small_recv) = refs[34:40]
-    (d_send, d_recv, g_send, g_recv, dx_send, dx_recv, load_sem) = refs[40:47]
+def layer_kernel(rows_n, paths, late_paths, links, *refs):
+    vector_refs, refs = refs[:9], refs[9:]
+    (x_in, cot, segments, q_in, k_in, v_in, w_out_in, w_up_in, w_down_in) = refs[:9]
+    refs = refs[:2] + refs[1:]
+    (q_out, k_out, v_out, o_out, up_out, down_out, qkv_kept, turned_kept) = refs[10:18]
+    (result, dx_out, small_out) = refs[18:21]
+    (x_all, mixed, w_out, w_up, w_down, w_own, w_mate, lse, seg_row, seg_wide) = refs[21:31]
+    (d_all, chip, dx_give, dx_land, gives, total, late_total, landing, late_land) = refs[31:40]
+    (small_land, send_sem, recv_sem, copy_sem, small_send, small_recv) = refs[40:46]
+    (x_send, x_recv, m_send, m_recv, d_send, d_recv) = refs[46:52]
+    (g_send, g_recv, dx_send, dx_recv, load_sem, own_sem, vecs) = refs[52:59]
+    d_give = mixed
     place = Place()
     me = place.pos
     mate, across = flip(me, 1), flip(me, 2)
-    peers = [across, flip(mate, 2), mate]
+    far = flip(mate, 2)
+    peers = [across, far, mate]
     core = bit_of(me, 1)
     tokens_n, features = x_in.shape
     part = tokens_n // rows_n
     length = 4 * part
     width = d_all.shape[1]
     heads = width // HEAD_DIM
-    inner_n = up_bias.shape[1]
+    inner_n = w_up.shape[1]
     half = features // 2
     quarters = inner_n // features
     outs = [window(down_out, j * features, features, 0, features) for j in range(inner_n // features)]
@@ -481,26 +360,162 @@
         chunk.advance()
         total[index] = keep().astype(LOW)
 
-    greet([place.partner(link) for link in links] + [(place.row, flip(mate, 2))])
+    to_across, to_mate, passed, own, m_copies = [], [], [], [], []
+
+    def x_spot(r, owner):
+        return rows_at(x_all, r * length + owner * part, part)
+
+    for r in range(rows_n):
+        src = x_in.at[pl.ds(r * part, part)]
+        x_sems = (x_send, x_recv)
+        to_across.append(remote(src, x_spot(r, me), x_sems, (0, r), (place.row, across)))
+        to_mate.append(remote(src, x_spot(r, me), x_sems, (1, r), (place.row, mate)))
+        spot = x_spot(r, across)
+        passed.append(remote(spot, spot, x_sems, (2, r), (place.row, mate)))
+        own.append(pltpu.make_async_copy(src, x_spot(r, me), own_sem.at[r]))
+        own[r].start()
+    weights = [
+        pltpu.make_async_copy(src, dst, load_sem.at[index])
+        for index, (src, dst) in enumerate(((w_out_in, w_out), (w_up_in, w_up), (w_down_in, w_down)))
+    ]
+    greet([place.partner(link) for link in links] + [(place.row, far)])
+    for r in range(rows_n):
+        to_across[r].start()
+        to_mate[r].start()
     give_at = pl.ds(pl.multiple_of((1 - core) * half, LANES), half)
     keep_at = pl.ds(pl.multiple_of(core * half, LANES), half)
     small_out[...] = jnp.zeros_like(small_out)
 
-    def dense(w_out, w_up, w_down, joined, hat, spread_one, low, turned, active, slope, d_low, d_up):
+    def attend(windows, qkv, x_turned, blend, lse_cols):
+        loads = []
+        for owner in range(2):
+            first = lax.div(3 * (me if owner == 0 else mate), 2) * LANES
+            for index, src in enumerate((q_in, k_in, v_in)):
+                at = 3 * owner + index
+                window_of = src.at[:, pl.ds(pl.multiple_of(first, LANES), TILE)]
+                loads.append(pltpu.make_async_copy(window_of, windows.at[at], load_sem.at[3 + at]))
+                loads[-1].start()
+        for copy in weights:
+            copy.start()
+        for index, ref in enumerate(vector_refs[:8]):
+            vecs[index : index + 1, :] = ref[...].astype(F32)[None]
+        up_bias = vector_refs[8][...].astype(F32)[None]
+        for quarter in range(quarters):
+            at = slice(quarter * features, (quarter + 1) * features)
+            vecs[8 + quarter : 9 + quarter, :] = up_bias[:, at]
+        seg_row[...] = segments[...].astype(F32)
+        for r in range(rows_n):
+            row = seg_row[r : r + 1, :]
+            seg_wide[r] = jnp.transpose(jnp.broadcast_to(row, (LANES, length)))
+        for load in loads:
+            load.wait()
+        for owner, dst in enumerate((w_own, w_mate)):
+            for index in range(3):
+                at = slice(index * width, (index + 1) * width)
+                for odd in range(2):
+
+                    @pl.when(lax.rem(me + owner, 2) == odd)
+                    def _():
+                        left = odd * HEAD_DIM
+                        dst[:, at] = windows[3 * owner + index, :, left : left + width]
+
+        first = pl.ds(pl.multiple_of(lax.div(3 * me, 2) * LANES, LANES), TILE)
+        odd = lax.rem(me, 2) == 1
+        biases = []
+        for index in range(2):
+            bias = vecs[index : index + 1, first]
+            biases.append(jnp.where(odd, bias[:, HEAD_DIM : HEAD_DIM + width], bias[:, :width]))
+        b_own = jnp.concatenate([biases[0], jnp.zeros((1, width), F32), biases[1]], axis=1)
+        is_query = lax.broadcasted_iota(jnp.int32, (1, 3 * width), 1) < width
+        scale = jnp.where(is_query, SCALE, 1.0)
+        kept = []
+        for r in range(rows_n):
+            to_across[r].wait_recv()
+            passed[r].start()
+            to_mate[r].wait_recv()
+            own[r].wait()
+            passed[r].wait_recv()
+            base = r * length
+            x_row = x_all[base : base + length, :]
+            made = ((dot(x_row, w_own[...]) + b_own) * scale).astype(LOW)
+            for index in range(3 * heads):
+                left = index * HEAD_DIM
+                qkv[index, base : base + length, :] = made[:, left : left + HEAD_DIM]
+            row = pl.ds(base, length)
+            kept.append(
+                pltpu.make_async_copy(qkv.at[:, row, :], qkv_kept.at[:, row, :], own_sem.at[r])
+            )
+            kept[-1].start()
+
+            @pl.loop(0, length // LANES)
+            def _(block):
+                here = pl.ds(pl.multiple_of(base + block * LANES, LANES), LANES)
+                local = pl.ds(pl.multiple_of(block * LANES, LANES), LANES)
+                seg_q = seg_wide[r, local, :]
+                same = jnp.concatenate([seg_q] * (length // LANES), axis=1) == seg_row[r : r + 1, :]
+                for head in range(heads):
+                    query = qkv[head, here, :]
+                    key = qkv[heads + head, base : base + length, :]
+                    value = qkv[2 * heads + head, base : base + length, :]
+                    scores = jnp.where(same, dot_nt(query, key), MASKED)
+                    top = jnp.max(scores, axis=-1, keepdims=True)
+                    power = jnp.exp(scores - top)
+                    sums = jnp.sum(power, axis=-1, keepdims=True)
+                    out = dot(power.astype(LOW), value) / sums
+                    blend[here, head * HEAD_DIM : (head + 1) * HEAD_DIM] = out.astype(LOW)
+                    column = r * heads + head
+                    lse_cols[local, column : column + 1] = top + jnp.log(sums)
+
+            for index, peer in enumerate(peers):
+                copy = remote(
+                    rows_at(blend, base + peer * part, part),
+                    mixed.at[me, pl.ds(r * part, part)],
+                    (m_send, m_recv),
+                    (index, r),
+                    (place.row, peer),
+                )
+                copy.start()
+                m_copies.append(copy)
+            mixed[me, r * part : (r + 1) * part, :] = blend[
+                pl.ds(pl.multiple_of(base + me * part, 16), part), :
+            ]
+        lse[...] = jnp.transpose(lse_cols[...])[: lse.shape[0], :]
+        mine_half = pl.ds(pl.multiple_of(core * half, LANES), half)
+        for r in range(rows_n):
+            base = r * length
+            x_turned[:, base : base + length] = jnp.transpose(x_all[base : base + length, mine_half])
+        kept.append(pltpu.make_async_copy(x_turned, turned_kept, own_sem.at[rows_n]))
+        kept[-1].start()
+        for copy in to_across + to_mate + passed:
+            copy.wait_send()
+        for copy in m_copies:
+            copy.wait()
+        for copy in kept:
+            copy.wait()
+
+    every = rows_n * length
+    pl.run_scoped(
+        attend,
+        pltpu.VMEM((6, features, TILE), LOW),
+        pltpu.VMEM(qkv_kept.shape, LOW),
+        pltpu.VMEM(turned_kept.shape, LOW),
+        pltpu.VMEM((every, width), LOW),
+        pltpu.VMEM((length, LANES), F32),
+    )
+
+    active = x_all
+
+    def dense(joined, hat, spread_one, low, turned, slope, d_low, d_up):
         acc = dx_out
-        loads = []
-        for index, (src, dst) in enumerate(((w_out_in, w_out), (w_up_in, w_up), (w_down_in, w_down))):
-            loads.append(pltpu.make_async_copy(src, dst, load_sem.at[index]))
-            loads[-1].start()
         for group in range(4):
             joined[:, group * width : (group + 1) * width] = mixed[group]
-        gain_one, shift_one = vecs[1:2, :], vecs[2:3, :]
-        gain_two, shift_two = vecs[4:5, :], vecs[5:6, :]
-        loads[0].wait()
+        gain_one, shift_one = vecs[3:4, :], vecs[4:5, :]
+        gain_two, shift_two = vecs[6:7, :], vecs[7:8, :]
+        weights[0].wait()
         acc[...] = dot(joined[...], w_out[...])
 
         def norm_one(at, carry):
-            v = x_in[at, :].astype(F32) + (acc[at, :] + vecs[0:1, :])
+            v = x_in[at, :].astype(F32) + (acc[at, :] + vecs[2:3, :])
             centred = v - jnp.mean(v, axis=-1, keepdims=True)
             over = lax.rsqrt(jnp.mean(centred * centred, axis=-1, keepdims=True) + EPS)
             v = centred * over
@@ -510,28 +525,36 @@
             return carry
 
         bands(tokens_n, 0, norm_one)
-        loads[1].wait()
-
-        @pl.loop(0, inner_n // TILE)
-        def _(tile):
-            cols = pl.ds(pl.multiple_of(tile * TILE, TILE), TILE)
-            u = dot(low[...], w_up[:, cols]) + up_bias[:, cols]
-            for band in range(tokens_n // BAND):
-                at = slice(band * BAND, (band + 1) * BAND)
-                g, s = gelu_and_slope(u[at])
-                active[at, cols] = g.astype(LOW)
-                slope[at, cols] = s
-
-        loads[2].wait()
+        weights[1].wait()
+        for quarter in range(quarters):
+
+            @pl.loop(0, features // TILE)
+            def _(tile):
+                cols = pl.ds(pl.multiple_of(tile * TILE, TILE), TILE)
+                wide = pl.ds(pl.multiple_of(quarter * features + tile * TILE, TILE), TILE)
+                u = dot(low[...], w_up[:, wide]) + vecs[8 + quarter : 9 + quarter, cols]
+                for band in range(tokens_n // BAND):
+                    at = slice(band * BAND, (band + 1) * BAND)
+                    g, s = gelu_and_slope(u[at])
+                    active[quarter * tokens_n + band * BAND : quarter * tokens_n + (band + 1) * BAND, cols] = g.astype(LOW)
+                    slope[at, wide] = s
+
+        weights[2].wait()
 
         @pl.loop(0, features // TILE)
         def _(tile):
             cols = pl.ds(pl.multiple_of(tile * TILE, TILE), TILE)
-            acc[:, cols] = dot(active[...], w_down[:, cols])
+            acc[:, cols] = sum(
+                dot(
+                    active[quarter * tokens_n : (quarter + 1) * tokens_n, :],
+                    w_down[quarter * features : (quarter + 1) * features, cols],
+                )
+                for quarter in range(quarters)
+            )
 
         def norm_two(at, carry):
             d_gain, d_shift, d_bias = carry
-            v = hat[at, :] * gain_one + shift_one + (acc[at, :] + vecs[3:4, :])
+            v = hat[at, :] * gain_one + shift_one + (acc[at, :] + vecs[5:6, :])
             centred = v - jnp.mean(v, axis=-1, keepdims=True)
             over = lax.rsqrt(jnp.mean(centred * centred, axis=-1, keepdims=True) + EPS)
             v = centred * over
@@ -553,11 +576,10 @@
             small_out[index : index + 1, :] = jnp.sum(value, axis=0, keepdims=True)
 
         for quarter in range(quarters):
-            first = quarter * features
 
             def some_down(side):
-                at = pl.ds(pl.multiple_of(first + side * half, LANES), half)
-                return dot_tn(active[:, at], d_low[...])
+                at = pl.ds(pl.multiple_of(side * half, LANES), half)
+                return dot_tn(active[quarter * tokens_n : (quarter + 1) * tokens_n, at], d_low[...])
 
             new_chunk(quarter, lambda: some_down(1 - core), lambda: some_down(core))
             tick()
@@ -616,25 +638,21 @@
     square = (tokens_n, features)
     pl.run_scoped(
         dense,
-        pltpu.VMEM((features, features), LOW),
-        pltpu.VMEM((features, inner_n), LOW),
-        pltpu.VMEM((inner_n, features), LOW),
         pltpu.VMEM(square, LOW),
         pltpu.VMEM(square, F32),
         pltpu.VMEM((tokens_n, LANES), F32),
         pltpu.VMEM(square, LOW),
         pltpu.VMEM((features, tokens_n), LOW),
-        pltpu.VMEM((tokens_n, inner_n), LOW),
         pltpu.VMEM((tokens_n, inner_n), F32),
         pltpu.VMEM(square, LOW),
         pltpu.VMEM(square, LOW),
     )
-
-    def attention(qkv, x_turned, w_own, w_mate, d_heads, prob, d_score):
+    prob = [w_up.at[pl.ds(0, length), pl.ds(head * length, length)] for head in range(heads)]
+    d_score = [w_down.at[pl.ds(head * features, length), pl.ds(0, length)] for head in range(heads)]
+
+    def attention(qkv, x_turned, d_heads):
         loads = []
-        for index, (src, dst) in enumerate(
-            ((qkv_in, qkv), (turned_in, x_turned), (w_own_in, w_own), (w_mate_in, w_mate))
-        ):
+        for index, (src, dst) in enumerate(((qkv_kept, qkv), (turned_kept, x_turned))):
             loads.append(pltpu.make_async_copy(src, dst, load_sem.at[index]))
             loads[-1].start()
         for load in loads:
@@ -661,8 +679,8 @@
                     p = jnp.exp(jnp.where(same, dot_nt(key, query) - log_total, MASKED))
                     dp = dot_nt(value, d_heads[head, local, :])
                     inner = jnp.sum(dp * p, axis=0, keepdims=True)
-                    prob[head, :, local] = p.astype(LOW)
-                    d_score[head, :, local] = (p * (dp - inner)).astype(LOW)
+                    prob[head][:, local] = p.astype(LOW)
+                    d_score[head][:, local] = (p * (dp - inner)).astype(LOW)
 
             blocks = length // LANES
             pl.loop(0, blocks // 2)(scores)
@@ -672,7 +690,7 @@
             for head in range(heads):
                 query = qkv[head, base : base + length, :]
                 key = qkv[heads + head, base : base + length, :]
-                ds = d_score[head]
+                ds = d_score[head][...]
                 at = slice(base, base + length)
                 left = head * HEAD_DIM
                 dq = dot_tn(ds, key) * SCALE
@@ -680,7 +698,7 @@
                 left += width
                 mine[at, left : left + HEAD_DIM] = dot(ds, query).astype(LOW)
                 left += width
-                mine[at, left : left + HEAD_DIM] = dot(prob[head], d_heads[head]).astype(LOW)
+                mine[at, left : left + HEAD_DIM] = dot(prob[head][...], d_heads[head]).astype(LOW)
             g_copies[r].start()
             tick()
 
@@ -701,10 +719,10 @@
             chunks[2 * quarters + 1 + index].advance()
             tick()
         token_sums = jnp.sum(mine[...].astype(F32), axis=0, keepdims=True)
-        group = lax.broadcasted_iota(jnp.int32, (4, 3 * width), 0)
-        spread = jnp.where(group == me, token_sums, 0.0)
-        spread = jnp.concatenate([spread, jnp.zeros((4, features - 3 * width), F32)], axis=1)
-        small_out[8:12, :] = spread
+        owner = lax.div(lax.broadcasted_iota(jnp.int32, (1, features), 1), width)
+        for row, left in ((8, 0), (9, 2 * width)):
+            spread = jnp.concatenate([token_sums[:, left : left + width]] * 4, axis=1)
+            small_out[row : row + 1, :] = jnp.where(owner == me, spread, 0.0)
         for r in range(rows_n):
             at = pl.ds(r * part, part)
             dx_out[at, :] += dx_of(r, me)
@@ -712,13 +730,9 @@
 
     pl.run_scoped(
         attention,
-        pltpu.VMEM(qkv_in.shape, LOW),
-        pltpu.VMEM(turned_in.shape, LOW),
-        pltpu.VMEM(w_own_in.shape, LOW),
-        pltpu.VMEM(w_mate_in.shape, LOW),
+        pltpu.VMEM(qkv_kept.shape, LOW),
+        pltpu.VMEM(turned_kept.shape, LOW),
         pltpu.VMEM((heads, length, HEAD_DIM), LOW),
-        pltpu.VMEM((heads, length, length), LOW),
-        pltpu.VMEM((heads, length, length), LOW),
     )
     smalls = [
         remote(
@@ -754,17 +768,17 @@
         copy.wait_send()
 
 
-def attend_rest(mesh_shape, x_rows, mixed, cot, vecs, up_bias, lse, seg_wide, seg_row, qkv, x_turned, w_out, w_up, w_down, w_own, w_mate):
+def layer(mesh_shape, vectors, x_rows, cot, segments, weights):
     row_bits = [("r", bit) for bit in axis_bits(mesh_shape["rows"])]
     pos_bits = [("p", bit) for bit in axis_bits(mesh_shape["pos"])]
     name = dict(zip("cyxzw", pos_bits + row_bits))
     paths = [[name[letter] for letter in path] + row_bits[3:] for path in PATHS]
     late_paths = [row_bits[3:][::-1] + [name[letter] for letter in path] for path in LATE_PATHS]
     links = pos_bits + row_bits
-    rows_n, length = seg_row.shape
+    rows_n, length = segments.shape
     tokens_n, features = x_rows.shape
-    inner_n = w_up.shape[1]
-    width = mixed.shape[2]
+    inner_n = weights[4].shape[1]
+    width = features // 4
     every = rows_n * length
     steps = len(links)
     half = features // 2
@@ -773,24 +787,36 @@
     vmem = pl.BlockSpec(memory_space=pltpu.VMEM)
     hbm = pl.BlockSpec(memory_space=pl.ANY)
     dma = pltpu.SemaphoreType.DMA
-    square = jax.ShapeDtypeStruct((features, features), LOW)
+    shape = jax.ShapeDtypeStruct
+    square = shape((features, features), LOW)
     return pl.pallas_call(
-        partial(rest_kernel, rows_n, paths, late_paths, links),
+        partial(layer_kernel, rows_n, paths, late_paths, links),
         out_shape=[
             square,
             square,
             square,
             square,
-            jax.ShapeDtypeStruct(w_up.shape, LOW),
-            jax.ShapeDtypeStruct(w_down.shape, LOW),
-            jax.ShapeDtypeStruct((tokens_n, features), LOW),
-            jax.ShapeDtypeStruct((tokens_n, features), F32),
-            jax.ShapeDtypeStruct((16, features), F32),
+            shape((features, inner_n), LOW),
+            shape((inner_n, features), LOW),
+            shape((3 * width // HEAD_DIM, every, HEAD_DIM), LOW),
+            shape((half, every), LOW),
+            shape((tokens_n, features), LOW),
+            shape((tokens_n, features), F32),
+            shape((16, features), F32),
         ],
-        in_specs=[vmem] * 8 + [hbm] * 7,
-        out_specs=[hbm] * 6 + [vmem] * 3,
+        in_specs=[vmem] * 12 + [hbm] * 6,
+        out_specs=[hbm] * 8 + [vmem] * 3,
         scratch_shapes=[
+            pltpu.VMEM((every, features), LOW),
             pltpu.VMEM((4, tokens_n, width), LOW),
+            pltpu.VMEM((features, features), LOW),
+            pltpu.VMEM((features, inner_n), LOW),
+            pltpu.VMEM((inner_n, features), LOW),
+            pltpu.VMEM((features, 3 * width), LOW),
+            pltpu.VMEM((features, 3 * width), LOW),
+            pltpu.VMEM((16, length), F32),
+            pltpu.VMEM((rows_n, length), F32),
+            pltpu.VMEM((rows_n, length, LANES), F32),
             pltpu.VMEM((every, width), LOW),
             pltpu.VMEM((2, every, 3 * width), LOW),
             pltpu.VMEM((tokens_n, features), LOW),
@@ -806,13 +832,11 @@
             dma((12,)),
             dma((steps,)),
             dma((steps,)),
-            dma((3, rows_n)),
-            dma((3, rows_n)),
-            dma((rows_n,)),
-            dma((rows_n,)),
-            dma((rows_n,)),
-            dma((rows_n,)),
-            dma((4,)),
+            *[dma((3, rows_n))] * 6,
+            *[dma((rows_n,))] * 4,
+            dma((9,)),
+            dma((rows_n + 1,)),
+            pltpu.VMEM((16, features), F32),
         ],
         compiler_params=pltpu.CompilerParams(
             collective_id=0, has_side_effects=True, vmem_limit_bytes=VMEM_LIMIT
@@ -820,33 +844,41 @@
         cost_estimate=pl.CostEstimate(
             flops=4 * 10**10, bytes_accessed=8 * 10**7, transcendentals=8 * 10**6
         ),
-        name="attend_rest",
-    )(x_rows, mixed, cot, vecs, up_bias, lse, seg_wide, seg_row, qkv, x_turned, w_out, w_up, w_down, w_own, w_mate)
-
-
-def widen_kernel(*refs):
-    half = len(refs) // 2
-    for src, dst in zip(refs[:half], refs[half:]):
-        dst[...] = src[...].astype(F32)
-
-
-def widen(arrays, steps):
+        name="layer",
+    )(*vectors, x_rows, cot, segments, *weights)
+
+
+def finish_kernel(moved, *refs):
+    sources = refs[: moved + 1]
+    outs = refs[moved + 1 :]
+    for src, dst in zip(sources[:moved], outs[:moved]):
+        dst[...] = src[...].astype(dst.dtype)
+    small = sources[moved]
+    for index, dst in enumerate(outs[moved:-1]):
+        dst[...] = small[index, :]
+    outs[-1][...] = jnp.concatenate([small[index, :] for index in range(12, 16)])
+
+
+def finish(blocks, result, grad_tokens, small, steps):
+    arrays = [*blocks, result, grad_tokens]
+    kinds = [F32] * len(blocks) + [result.dtype, grad_tokens.dtype]
     specs = [pl.BlockSpec((a.shape[0] // steps, a.shape[1]), lambda i: (i, 0)) for a in arrays]
-    moved = sum(6 * a.size for a in arrays)
+    features = small.shape[1]
+    vectors = [features] * 10 + [4 * features]
+    shape = jax.ShapeDtypeStruct
     return pl.pallas_call(
-        widen_kernel,
+        partial(finish_kernel, len(arrays)),
         grid=(steps,),
-        out_shape=[jax.ShapeDtypeStruct(a.shape, F32) for a in arrays],
-        in_specs=specs,
-        out_specs=specs,
+        out_shape=[shape(a.shape, kind) for a, kind in zip(arrays, kinds)]
+        + [shape((size,), F32) for size in vectors],
+        in_specs=[*specs, pl.BlockSpec(small.shape, lambda i: (0, 0))],
+        out_specs=[*specs, *[pl.BlockSpec((size,), lambda i: (0,)) for size in vectors]],
         compiler_params=pltpu.CompilerParams(vmem_limit_bytes=VMEM_LIMIT),
-        cost_estimate=pl.CostEstimate(flops=0, bytes_accessed=moved, transcendentals=0),
-        name="widen",
-    )(*arrays)
-
-
-def own_columns(w, index, width):
-    return lax.dynamic_slice_in_dim(w, index * width, width, w.ndim - 1)
+        cost_estimate=pl.CostEstimate(
+            flops=0, bytes_accessed=6 * sum(a.size for a in arrays), transcendentals=0
+        ),
+        name="finish",
+    )(*arrays, small)
 
 
 def on_device(
@@ -871,68 +903,38 @@
     cotangent,
 ):
     rows_n, part_len, features = tokens.shape
-    length = segments.shape[1]
-    groups = mesh_shape["pos"]
-    width = features // groups
-    here = lax.axis_index("pos")
-    mate = here + 1 - 2 * lax.rem(here, 2)
-    x_rows = tokens.reshape(rows_n * part_len, features)
-    seg_row = segments.astype(F32)
-    seg_wide = jnp.broadcast_to(seg_row[:, :, None], (rows_n, length, LANES))
-
-    def heads_of(index):
-        return jnp.concatenate(
-            [own_columns(w, index, width) for w in (w_query, w_key, w_value)], axis=1
-        )
-
-    w_own, w_mate = heads_of(here), heads_of(mate)
-    b_own = jnp.concatenate(
-        [
-            own_columns(b_query.astype(F32), here, width),
-            jnp.zeros((width,), F32),
-            own_columns(b_value.astype(F32), here, width),
-        ]
-    )[None]
-    x_turned, qkv, lse, mixed = attend_forward(x_rows, w_own, b_own, seg_wide, seg_row, rows_n)
-    vecs = jnp.stack([b_out, gain_one, shift_one, b_down, gain_two, shift_two]).astype(F32)
-    *blocks, result, grad_tokens, small = attend_rest(
+    flat = (rows_n * part_len, features)
+    vectors = (b_query, b_value, b_out, gain_one, shift_one, b_down, gain_two, shift_two, b_up)
+    outs = layer(
         mesh_shape,
-        x_rows,
-        mixed,
-        cotangent.reshape(rows_n * part_len, features),
-        jnp.pad(vecs, ((0, 2), (0, 0))),
-        b_up.astype(F32)[None],
-        lse,
-        seg_wide,
-        seg_row,
-        qkv,
-        x_turned,
-        w_out,
-        w_up,
-        w_down,
-        w_own,
-        w_mate,
+        vectors,
+        tokens.reshape(flat),
+        cotangent.reshape(flat),
+        segments,
+        (w_query, w_key, w_value, w_out, w_up, w_down),
     )
-    grad_w_query, grad_w_key, grad_w_value, grad_w_out, grad_w_up, grad_w_down = widen(blocks, 12)
+    (g_query, g_key, g_value, g_out, g_up, g_down, result, grad_tokens, *vectors) = finish(
+        outs[:6], *outs[8:], 6
+    )
     shape = (rows_n, part_len, features)
     return (
         result.reshape(shape),
         grad_tokens.reshape(shape),
-        grad_w_query,
-        small[8:12, :width].reshape(-1),
-        grad_w_key,
-        grad_w_value,
-        small[8:12, 2 * width : 3 * width].reshape(-1),
-        grad_w_out,
-        small[0],
-        small[1],
-        small[2],
-        grad_w_up,
-        small[12:16].reshape(-1),
-        grad_w_down,
-        small[3],
-        small[4],
-        small[5],
+        g_query,
+        vectors[8],
+        g_key,
+        g_value,
+        vectors[9],
+        g_out,
+        vectors[0],
+        vectors[1],
+        vectors[2],
+        g_up,
+        vectors[10],
+        g_down,
+        vectors[3],
+        vectors[4],
+        vectors[5],
     )
 
 

time: 242 us -> 213 us (0.88)
  local copies, waits for them, and re-layouts: 17.9 us -> 0 us
  other arithmetic: 5.28 us -> 0 us
  Pallas kernels: 214 us -> 210 us
    pallas_call x3 -> x2, Pallas kernels: 214 us -> 210 us  [the longest x1 193 us: layer(): pl.pallas_call(partial(layer_kernel, rows_n, paths, late_paths, links), o...]
    another operation x7 -> x0, local copies, waits for them, and re-layouts: 4.15 us -> none  [on_device(): jnp.stack([b_out, gain_one, shift_one, b_down, gain_two, shift_two])]
    dynamic_slice x4 -> x0, local copies, waits for them, and re-layouts: 4.03 us -> none  [own_columns(): return lax.dynamic_slice_in_dim(w, index * width, width, w.ndim - 1)]
    slice x3 -> x0, local copies, waits for them, and re-layouts: 3.2 us -> none  [the longest x1 1.74 us: on_device(): small[5]]
    unnamed x12 -> x0, local copies, waits for them, and re-layouts: 2.75 us -> none
    concatenate x3 -> x0, other arithmetic: 2.67 us -> none  [the longest x2 2.59 us: heads_of(): jnp.concatenate([own_columns(w, index, width) for w in (w_query, w_key, w...]
where the time goes in v1:
time: 213 us; the launch traced here: 211 us
  Pallas kernels  210 us (99%)
    pallas_call x1, Pallas kernels, layer(): pl.pallas_call(partial(layer_kernel, rows_n, paths, late_paths, links), o...  193 us
    pallas_call x1, Pallas kernels, finish(): pl.pallas_call(partial(finish_kernel, len(arrays)), grid=(steps,), out_sh...  17.3 us

profile of v1, /device:TPU:0, one launch (start us, length us, event | category | flops | bytes accessed | tf_op | source)
XLA Modules:
  0.0 210.7 jit_solution(8697219494192608208)
XLA Ops:
  0.7 192.5 %layer.1 = (bf16[768,768]{1,0:T(8,128)(2,1)}, bf16[768,768]{1,0:T(8,128)(2,1)}, bf16[768,768]{1,0:T(8,128)(2,1)}, bf16[768,768]{1,0:T(8,128)(2,1)}, bf16[768,307...) custom-call(bf16[768]{0:T(1024)(128)(2,1)} %refs_0_.1, ...), custom_call_target="tpu_custom_call" | custom-call | flops 40000000000 | bytes 80000000 | tf_op jit(solution)/shard_map/layer/pallas_call | solution.py:792
  193.2 17.3 %finish.1 = (f32[768,768]{1,0:T(8,128)}, f32[768,768]{1,0:T(8,128)}, f32[768,768]{1,0:T(8,128)}, f32[768,768]{1,0:T(8,128)}, f32[768,3072]{1,0:T(8,128)}, /*inde...) custom-call(bf16[768,768]{1,0:T(8,128)(2,1)} %get-tuple-element.43.r, ...), custom_call_target="tpu_custom_call" | custom-call | bytes 46891008 | tf_op jit(solution)/shard_map/finish/pallas_call | solution.py:869
